TPU v7x, 256 devices: a whole 4x4x8 slice. The times are simulated.
256 devices in a mesh: noise: 8 (over z), row: 16 (over y, x), col: 2 (over core).
Axes of the slice: x: 4, y: 4, z: 8, core: 2. Of those that a mesh axis runs over, the one named last changes fastest.
Arguments:
- images: bfloat16 [256, 4, 6144], P('row', None, 'col'), may hold values from -40 to 40
- gain: float32 [6144], P('col'), may hold values from 0.3 to 3.5
- up_weight: bfloat16 [6144, 12288], P('col', 'row'), may hold values from -0.078125 to 0.078125
- down_weight: bfloat16 [12288, 6144], P('row', 'col'), may hold values from -0.0546875 to 0.0546875
- cotangent: bfloat16 [256, 16, 6144], P('row', 'noise', 'col'), may hold values from -6 to 6
- seeds: int32 [16], P('noise'), may hold values from 0 to 999999
- assign: int32 [16, 1], replicated, may hold values from 0 to 3, as said below
Outputs:
- saliency: float32 [256, 4, 6144], P('row', None, 'col')
Inputs may be any that keep to these rules, and one draw needn't show every extreme that they name: `assign`: every one of the 4 images is named by at least one copy.
All inputs are finite; a program needn't handle non-finite values.
Results may differ from a plain program's by a relative error of at most 0.0019.
Values may be sent and summed in bfloat16 or wider, within the bound.
A program may use at most 64 MiB of HBM per device.

v0:
```python
import math
import jax
import jax.numpy as jnp
from jax import lax
from jax.sharding import PartitionSpec as P

D = 6144
noise_scale = 0.6
gelu_coef = 0.044715
root_term = math.sqrt(2.0 / math.pi)


def mix_noise(seed_value, token_index, feature_index, width):
    linear = token_index[:, None] * width + feature_index[None, :]
    mixed = linear * 1664525 + seed_value * 1013904223
    mixed = mixed ^ mixed >> 13
    mixed = mixed * 1274126177
    mixed = mixed ^ mixed >> 16
    return ((mixed & 65535).astype(jnp.float32) - 32767.5) * (1.0 / 18918.0)


def gelu_slope(preact):
    inner = root_term * (preact + gelu_coef * preact * preact * preact)
    tanh_val = jnp.tanh(inner)
    return 0.5 * (1.0 + tanh_val) + 0.5 * preact * (1.0 - tanh_val * tanh_val) * root_term * (
        1.0 + 3.0 * gelu_coef * preact * preact
    )


def body(images, gain, up_weight, down_weight, cotangent, seeds, assign):
    tok_local = images.shape[0]
    image_count = images.shape[1]
    width_local = images.shape[2]
    planes = lax.axis_size("noise")
    rows = lax.axis_size("row")
    part = tok_local // planes
    col_index = lax.axis_index("col")
    row_index = lax.axis_index("row")
    noise_index = lax.axis_index("noise")
    all_seeds = lax.all_gather(seeds, "noise", tiled=True)
    slots = all_seeds.shape[0]
    own_cot = lax.all_to_all(cotangent, "noise", split_axis=0, concat_axis=1, tiled=True)
    own_images = lax.dynamic_slice_in_dim(images, noise_index * part, part)
    plane_images = lax.all_gather(own_images, "row", axis=0, tiled=True)
    plane_cot = lax.all_gather(own_cot, "row", axis=0, tiled=True)
    image_ids = jnp.arange(image_count, dtype=jnp.int32)
    onehot = (assign[:, 0][:, None] == image_ids[None, :]).astype(jnp.float32)
    counts = jnp.sum(onehot, axis=0)
    clean = jnp.einsum(
        "si,tid->tsd", onehot.astype(jnp.bfloat16), plane_images, preferred_element_type=jnp.float32
    )
    tokens = (
        jnp.arange(rows, dtype=jnp.int32)[:, None] * tok_local
        + noise_index * part
        + jnp.arange(part, dtype=jnp.int32)[None, :]
    ).reshape(-1)
    feature_index = col_index * width_local + jnp.arange(width_local, dtype=jnp.int32)
    noise_field = jax.vmap(
        lambda seed_value: mix_noise(seed_value, tokens, feature_index, D), out_axes=1
    )(all_seeds)
    noisy = clean + noise_scale * noise_field
    feat_mean = lax.psum(jnp.sum(noisy, axis=-1), "col") / D
    centred = noisy - feat_mean[..., None]
    feat_var = lax.psum(jnp.sum(centred * centred, axis=-1), "col") / D
    inv_std = lax.rsqrt(feat_var + 1e-06)
    normed = centred * inv_std[..., None]
    scaled = (normed * gain).astype(jnp.bfloat16)
    n = tokens.shape[0] * slots
    preact_part = jnp.dot(
        scaled.reshape(n, width_local), up_weight, preferred_element_type=jnp.float32
    )
    back_part = jnp.einsum(
        "td,hd->th",
        plane_cot.reshape(n, width_local),
        down_weight,
        preferred_element_type=jnp.float32,
    )
    ug_part = jnp.sum(gain[:, None] * up_weight.astype(jnp.float32), axis=0)
    preact, back_grad, ug = lax.psum((preact_part, back_part, ug_part), "col")
    hidden_grad = (back_grad * gelu_slope(preact)).astype(jnp.bfloat16)
    hg = hidden_grad.astype(jnp.float32)
    sums = jnp.stack([jnp.sum(hg * ug, axis=-1), jnp.sum(hg * preact, axis=-1)], axis=-1) / D
    sums = lax.psum_scatter(sums.reshape(-1, slots, 2), "row", scatter_dimension=0, tiled=True)
    weighted = jnp.einsum(
        "ts,si,tsh->tih",
        inv_std,
        onehot,
        hg.reshape(-1, slots, hg.shape[-1]),
        precision=lax.Precision.HIGHEST,
    ).astype(jnp.bfloat16)
    grad = jnp.einsum(
        "th,dh->td",
        weighted.reshape(-1, hg.shape[-1]),
        up_weight,
        preferred_element_type=jnp.float32,
    )
    grad = lax.psum_scatter(
        grad.reshape(-1, image_count, width_local), "row", scatter_dimension=0, tiled=True
    )
    own_normed = lax.dynamic_slice_in_dim(normed, row_index * part, part)
    own_inv = lax.dynamic_slice_in_dim(inv_std, row_index * part, part)
    rest = own_cot.astype(jnp.float32) - own_inv[..., None] * (
        sums[..., 0][..., None] + own_normed * sums[..., 1][..., None]
    )
    total = grad * gain + jnp.einsum("si,tsd->tid", onehot, rest, precision=lax.Precision.HIGHEST)
    total = total / counts[None, :, None]
    return lax.all_gather(total, "noise", axis=0, tiled=True)


def solution(mesh):
    placed = (
        P("row", None, "col"),
        P("col"),
        P("col", "row"),
        P("row", "col"),
        P("row", "noise", "col"),
        P("noise"),
        P(),
    )
    return jax.shard_map(
        body, mesh=mesh, in_specs=placed, out_specs=P("row", None, "col"), check_vma=False
    )
```

profile of v0, /device:TPU:2, one launch (start us, length us, event | category | flops | bytes accessed | tf_op | source)
XLA Modules:
  0.0 281.2 jit_solution(14509511110187522334)
XLA Ops:
  6.5 0.0 copy-start
  6.5 0.0 all-gather.2.cloned.1.call-start
  6.5 19.1 %all_to_all.18 = bf16[16,2,3072]{2,1,0:T(2,128)(2,1)S(1)} all-to-all(bf16[16,2,3072]{2,1,0:T(2,128)(2,1)} %param.11), channel_id=1, replica_groups=mesh['noise'=8,'row'=16,'col'=2] {'noise'}, dimensions={0} | all-to-all | bytes 393216 | tf_op jit(solution)/shard_map/all_to_all | solution.py:42
  25.6 0.1 copy.26
  25.7 0.8 all_to_all.16
  26.5 0.0 all-gather.2.cloned.1.call-update
  26.5 0.0 all-reduce.10.cloned.1.call-start
  26.6 0.1 add_multiply_fusion.1
  26.7 0.1 mul.175
  26.8 1.3 dynamic-slice
  28.8 0.9 dynamic-update-slice
  29.7 10.1 %all-reduce = s32[16]{0:T(128)S(1)} all-reduce(s32[16]{0:T(128)S(1)} %dynamic-update-slice), channel_id=1, replica_groups=mesh['noise'=8,'row'=16,'col'=2] {'noise'}, use_global_device_ids=true, to_apply=%add | all-reduce | flops 16 | bytes 128
  39.8 0.0 copy-done
  39.8 25.4 %all_gather.12 = bf16[32,4,3072]{2,1,0:T(4,128)(2,1)S(1)} all-gather(bf16[2,4,3072]{2,1,0:T(4,128)(2,1)S(1)} %constant_dynamic-slice_fusion.1), channel_id=1, replica_groups=mesh['noise'=8,'row'=16,'col'=2] {'row'}, dimensions={0}, use_global_device_ids=true | all-gather | bytes 835584 | tf_op jit(solution)/shard_map/all_gather | solution.py:44
  65.2 0.1 add_multiply_fusion
  65.3 5.3 %fusion.44 = (f32[32,16]{1,0:T(8,128)S(1)}, f32[32,16,3072]{2,1,0:T(8,128)}) fusion(s32[16]{0:T(128)S(1)} %broadcast_multiply_fusion.1, s32[32,3072]{1,0:T(8,128)S(1)} %add_multiply_fusion, bf16[32,4,3072]{2,1,0:T(4,128)(2,1)S(1)} %all_gather.12, s32[16]{0:T(128)} %bitcast.49), kind=kOutput, calls=%fused_computation.68 | convolution fusion | flops 31456960 | bytes 7473280 | tf_op jit(solution)/shard_map/si,tid->tsd/dot_general | solution.py:49
  70.7 3.5 %psum.35 = f32[32,16]{1,0:T(8,128)S(1)} all-reduce(f32[32,16]{1,0:T(8,128)S(1)} %get-tuple-element.18), channel_id=1, replica_groups=mesh['noise'=8,'row'=16,'col'=2] {'col'}, use_global_device_ids=true, to_apply=%region_1.0 | all-reduce | flops 512 | bytes 4096 | tf_op jit(solution)/shard_map/psum | solution.py:62
  74.1 3.5 %multiply_reduce_fusion.1 = f32[32,16]{1,0:T(8,128)S(1)} fusion(f32[32,16,3072]{2,1,0:T(8,128)} %get-tuple-element.19, f32[32,16]{1,0:T(8,128)S(1)} %broadcast_multiply_fusion), kind=kLoop, calls=%fused_computation.10 | loop fusion | flops 4718080 | bytes 6295552 | tf_op jit(solution)/shard_map/reduce_sum | solution.py:64
  77.7 0.0 copy-done.2
  77.7 0.0 slice-start
  77.7 3.4 %multiply_reduce_fusion = f32[768]{0:T(1024)S(1)} fusion(bf16[3072,768]{1,0:T(8,128)(2,1)} %param.9, f32[3072]{0:T(1024)S(1)} %copy-done.2), kind=kLoop, calls=%fused_computation.2 | loop fusion | flops 7077120 | bytes 4733952 | tf_op jit(solution)/shard_map/reduce_sum | solution.py:78
  81.1 3.6 %all-reduce.3 = (f32[32,16]{1,0:T(8,128)S(1)}, f32[768]{0:T(1024)S(1)}) all-reduce(f32[32,16]{1,0:T(8,128)S(1)} %multiply_reduce_fusion.1, f32[768]{0:T(1024)S(1)} %multiply_reduce_fusion), channel_id=1, replica_groups=mesh['noise'=8,'row'=16,'col'=2] {'col'}, use_global_device_ids=true, to_apply=%region_3.0 | all-reduce | flops 1280 | bytes 10240 | tf_op jit(solution)/shard_map/psum | solution.py:64
  84.7 0.0 slice-start.1
  84.7 7.3 %multiply_convert_fusion = (bf16[32,16,3072]{2,1,0:T(8,128)(2,1)S(1)}, f32[32,16,3072]{2,1,0:T(8,128)}) fusion(f32[3072]{0:T(1024)S(1)} %copy-done.2, f32[32,16]{1,0:T(8,128)S(1)} %get-tuple-element.17, f32[32,16,3072]{2,1,0:T(8,128)} %get-tuple-element.19, f32[32,16]{1,0:T(8,128)S(1)} %broadcast_multiply_fusion), kind=kLoop, calls=%fused_computation.9 | loop fusion | flops 6291456 | bytes 15745024 | tf_op jit(solution)/shard_map/convert_element_type | solution.py:67
  92.0 0.0 slice-done
  92.0 0.0 slice-done.1
  92.0 3.8 %fusion.46 = f32[512,768]{1,0:T(8,128)} fusion(bf16[512,3072]{1,0:T(8,128)(2,1)S(1)} %bitcast.46, bf16[3072,768]{1,0:T(8,128)(2,1)S(1)} %bitcast.44), kind=kOutput, calls=%fused_computation.70 | convolution fusion | flops 2415919104 | bytes 9437184 | tf_op jit(solution)/shard_map/dot_general | solution.py:69
  95.8 7.1 %fusion.45 = f32[512,768]{1,0:T(8,128)} fusion(bf16[512,3072]{1,0:T(8,128)(2,1)} %bitcast.53, bf16[768,3072]{1,0:T(8,128)(2,1)} %param.10), kind=kOutput, calls=%fused_computation.69 | convolution fusion | flops 2415919104 | bytes 9437184 | tf_op jit(solution)/shard_map/td,hd->th/dot_general | solution.py:72
  102.9 0.0 all-reduce.10.cloned.1.call-update
  102.9 0.2 all-reduce.8.cloned.1.call-start
  103.2 31.5 %all-reduce.10.cloned.1.call-done = (f32[512,768]{1,0:T(8,128)}, f32[512,768]{1,0:T(8,128)}) async-done(((f32[512,768]{1,0:T(8,128)}, f32[512,768]{1,0:T(8,128)}), (f32[512,768]{1,0:T(8,128)}, f32[512,768]{1,0:T(8,128)})) %all-reduce.10.cloned.1.call-update) | async-done | bytes 3145744 | tf_op jit(solution)/shard_map/psum | solution.py:79
  134.7 3.2 %fusion.10 = (f32[512]{0:T(512)S(1)}, f32[512]{0:T(512)S(1)}, bf16[512,768]{1,0:T(8,128)(2,1)S(1)}) fusion(f32[768]{0:T(1024)S(1)} %get-tuple-element.8, f32[512,768]{1,0:T(8,128)} %get-tuple-element.10, f32[512,768]{1,0:T(8,128)} %get-tuple-element.9), kind=kLoop, calls=%fused_computation.21 | loop fusion | flops 9436160 | bytes 3939328 | tf_op jit(solution)/shard_map/reduce_sum | solution.py:82
  137.9 0.5 convolution_convert_fusion
  138.3 0.0 copy-start.4
  138.4 0.0 copy-start.1
  138.4 4.0 %fusion.6 = f32[32,4,3072]{2,0,1:T(8,128)S(1)} fusion(bf16[3072,768]{1,0:T(8,128)(2,1)} %param.9, bf16[32,4,768]{2,1,0:T(4,128)(2,1)S(1)} %convolution_convert_fusion), kind=kOutput, calls=%fused_computation.12 | convolution fusion | flops 603979776 | bytes 6488064 | tf_op jit(solution)/shard_map/th,dh->td/dot_general | solution.py:91
  142.4 2.2 copy.20
  144.6 0.0 all-reduce.8.cloned.1.call-update
  144.7 0.6 dynamic-slice.1
  145.9 0.1 fusion.35
  146.1 0.1 stack.10
  146.1 0.1 stack.9
  146.2 69.6 %all-reduce.2 = f32[32,16,2]{1,0,2:T(8,128)S(1)} all-reduce(f32[32,16,2]{1,0,2:T(8,128)S(1)} %maximum_multiply_fusion), channel_id=3, replica_groups=mesh['noise'=8,'row'=16,'col'=2] {'row'}, use_global_device_ids=true, to_apply=%region_11.0.clone | all-reduce | flops 1024 | bytes 8192
  215.9 28.8 %all-reduce.8.cloned.1.call-done = f32[32,4,3072]{2,1,0:T(4,128)} async-done(((f32[32,4,3072]{2,1,0:T(4,128)}), f32[32,4,3072]{2,1,0:T(4,128)}) %all-reduce.8.cloned.1.call-update) | async-done | bytes 1572880
  244.7 0.0 copy-done.1
  244.7 1.4 fusion.9
  246.1 27.8 %all_gather.15 = f32[16,4,3072]{2,1,0:T(4,128)S(1)} all-gather(f32[2,4,3072]{2,1,0:T(4,128)S(1)} %fusion.9), channel_id=1, replica_groups=mesh['noise'=8,'row'=16,'col'=2] {'noise'}, dimensions={0}, use_global_device_ids=true | all-gather | bytes 884736 | tf_op jit(solution)/shard_map/all_gather | solution.py:107
  273.8 0.9 copy.32
  (17 shorter events, 0.1 us)
Async XLA Ops:
  6.5 33.3 %copy-start = (bf16[16,4,3072]{2,1,0:T(4,128)(2,1)S(1)}, bf16[16,4,3072]{2,1,0:T(4,128)(2,1)}, u32[]{:S(2)}) copy-start(bf16[16,4,3072]{2,1,0:T(4,128)(2,1)} %param.7) | copy-start | bytes 1179652
  6.5 89.3 %all-gather.2.cloned.1.call-start = ((), (), s32[]{:S(2)}) async-start(), calls=%async_computation.1 | async-start | bytes 3342336 | tf_op jit(solution)/shard_map/all_gather | solution.py:45
  26.5 108.2 %all-reduce.10.cloned.1.call-start = ((), (), s32[]{:S(2)}) async-start(), calls=%async_computation.3 | async-start | bytes 6291456 | tf_op jit(solution)/shard_map/psum | solution.py:79
  70.7 7.0 %copy-start.2 = (f32[3072]{0:T(1024)S(1)}, f32[3072]{0:T(1024)}, u32[]{:S(2)}) copy-start(f32[3072]{0:T(1024)} %param.8) | copy-start | bytes 36868
  77.7 14.3 %slice-start = ((s8[4718592]{0:T(1024)(128)(4,1)}), s8[524288]{0:T(1024)(128)(4,1)S(1)}, s32[]{:S(2)}) async-start(s8[4718592]{0:T(1024)(128)(4,1)} %bitcast.43), calls=%async_computation.4 | async-start | bytes 1048576
  84.7 7.3 %slice-start.1 = ((s8[4718592]{0:T(1024)(128)(4,1)}), s8[4194304]{0:T(1024)(128)(4,1)S(1)}, s32[]{:S(2)}) async-start(s8[4718592]{0:T(1024)(128)(4,1)} %bitcast.43), calls=%async_computation.5 | async-start | bytes 8388608
  95.8 7.3 %copy-start.3 = (s32[16,1]{0,1:T(1,128)S(1)}, s32[16,1]{0,1:T(1,128)}, u32[]{:S(2)}) copy-start(s32[16,1]{0,1:T(1,128)} %param.13) | copy-start | bytes 196
  102.9 141.7 %all-reduce.8.cloned.1.call-start = ((), (), s32[]{:S(2)}) async-start(), calls=%async_computation.2 | async-start | bytes 3145728
  138.3 6.3 %copy-start.4 = (u32[256]{0:T(256)S(1)}, u32[256]{0:T(256)}, u32[]{:S(2)}) copy-start(u32[256]{0:T(256)} %constant.75) | copy-start | bytes 3076
  138.4 106.3 %copy-start.1 = (bf16[2,16,3072]{2,1,0:T(8,128)(2,1)S(1)}, bf16[2,16,3072]{2,1,0:T(8,128)(2,1)}, u32[]{:S(2)}) copy-start(bf16[2,16,3072]{2,1,0:T(8,128)(2,1)} %all_to_all.16) | copy-start | bytes 589828
Sparse Core Ops, SparseCore 0:
  26.6 49.4 all-gather.1
  103.0 31.6 all-reduce.9
  144.8 99.8 all-reduce.7
where the time goes:
time: 282 us; the launch traced here: 281 us
  blocking collectives  159 us (56%)
  waiting for transfers between devices  60.4 us (21%)
  matrix products  22.1 us (8%)
  other arithmetic  17.7 us (6%)
  between operations  14.6 us (5%)
  local copies, waits for them, and re-layouts  7.19 us (3%)
    unnamed x2, blocking collectives  79.7 us
    psum x1, waiting for transfers between devices, body(): preact, back_grad, ug = lax.psum((preact_part, back_part, ug_part), 'col')  31.5 us
    unnamed x4, waiting for transfers between devices  28.8 us
    all_gather x1, blocking collectives, body(): return lax.all_gather(total, 'noise', axis=0, tiled=True)  27.8 us
    all_gather x1, blocking collectives, body(): plane_images = lax.all_gather(own_images, 'row', axis=0, tiled=True)  25.4 us
    all_to_all x1, blocking collectives, body(): lax.all_to_all(cotangent, 'noise', split_axis=0, concat_axis=1, tiled=True)  19.1 us
    convert_element_type x1, other arithmetic, body(): scaled = (normed * gain).astype(jnp.bfloat16)  7.28 us
    dot_general x1, matrix products, body(): jnp.einsum('td,hd->th', plane_cot.reshape(n, width_local), down_weight, p...  7.09 us
  transfers between devices with their start and end apart: 3, of which 2 were waited for; matrix products, arithmetic and copies ran while one was open for 10% of the time, Pallas kernels for 0%

commit v1 on v0

--- a/solution.py
+++ b/solution.py
@@ -104,7 +104,9 @@
     )
     total = grad * gain + jnp.einsum("si,tsd->tid", onehot, rest, precision=lax.Precision.HIGHEST)
     total = total / counts[None, :, None]
-    return lax.all_gather(total, "noise", axis=0, tiled=True)
+    return jnp.concatenate(
+        lax.all_to_all(jnp.stack([total] * lax.axis_size("noise")), "noise", 0, 0), axis=0
+    )
 
 
 def solution(mesh):

time: 282 us -> 282 us (level)
    all_to_all x0 -> x1, blocking collectives: none -> 28.3 us  [body(): lax.all_to_all(jnp.stack([total] * lax.axis_size('noise')), 'noise', 0, 0)]
    all_gather x1 -> x0, blocking collectives: 27.8 us -> none  [body(): return lax.all_gather(total, 'noise', axis=0, tiled=True)]
where the time goes in v1:
time: 282 us
  blocking collectives  160 us (57%)
  waiting for transfers between devices  60.4 us (21%)
  matrix products  22.1 us (8%)
  other arithmetic  17.7 us (6%)
  between operations  14.6 us (5%)
  local copies, waits for them, and re-layouts  7.33 us (3%)
    unnamed x2, blocking collectives  79.7 us
    psum x1, waiting for transfers between devices, body(): preact, back_grad, ug = lax.psum((preact_part, back_part, ug_part), 'col')  31.5 us
    unnamed x4, waiting for transfers between devices  28.8 us
    all_to_all x1, blocking collectives, body(): lax.all_to_all(jnp.stack([total] * lax.axis_size('noise')), 'noise', 0, 0)  28.3 us
    all_gather x1, blocking collectives, body(): plane_images = lax.all_gather(own_images, 'row', axis=0, tiled=True)  25.4 us
    all_to_all x1, blocking collectives, body(): lax.all_to_all(cotangent, 'noise', split_axis=0, concat_axis=1, tiled=True)  19.1 us
    convert_element_type x1, other arithmetic, body(): scaled = (normed * gain).astype(jnp.bfloat16)  7.28 us
    dot_general x1, matrix products, body(): jnp.einsum('td,hd->th', plane_cot.reshape(n, width_local), down_weight, p...  7.09 us
  transfers between devices with their start and end apart: 3, of which 2 were waited for; matrix products, arithmetic and copies ran while one was open for 10% of the time, Pallas kernels for 0%

profile of v1, /device:TPU:2, one launch (start us, length us, event | category | flops | bytes accessed | tf_op | source)
XLA Modules:
  0.0 282.0 jit_solution(13066125752017076805)
XLA Ops:
  6.5 0.0 copy-start
  6.5 0.0 all-gather.2.cloned.1.call-start
  6.5 19.1 %all_to_all.23 = bf16[16,2,3072]{2,1,0:T(2,128)(2,1)S(1)} all-to-all(bf16[16,2,3072]{2,1,0:T(2,128)(2,1)} %param.11), channel_id=1, replica_groups=mesh['noise'=8,'row'=16,'col'=2] {'noise'}, dimensions={0} | all-to-all | bytes 393216 | tf_op jit(solution)/shard_map/all_to_all | solution.py:42
  25.6 0.1 copy.26
  25.7 0.8 all_to_all.19
  26.5 0.0 all-gather.2.cloned.1.call-update
  26.5 0.0 all-reduce.10.cloned.1.call-start
  26.6 0.1 add_multiply_fusion.1
  26.7 0.1 mul.175
  26.8 1.3 dynamic-slice
  28.8 0.9 dynamic-update-slice
  29.7 10.1 %all-reduce = s32[16]{0:T(128)S(1)} all-reduce(s32[16]{0:T(128)S(1)} %dynamic-update-slice), channel_id=1, replica_groups=mesh['noise'=8,'row'=16,'col'=2] {'noise'}, use_global_device_ids=true, to_apply=%add | all-reduce | flops 16 | bytes 128
  39.8 0.0 copy-done
  39.8 25.4 %all_gather.9 = bf16[32,4,3072]{2,1,0:T(4,128)(2,1)S(1)} all-gather(bf16[2,4,3072]{2,1,0:T(4,128)(2,1)S(1)} %constant_dynamic-slice_fusion.1), channel_id=1, replica_groups=mesh['noise'=8,'row'=16,'col'=2] {'row'}, dimensions={0}, use_global_device_ids=true | all-gather | bytes 835584 | tf_op jit(solution)/shard_map/all_gather | solution.py:44
  65.2 0.1 add_multiply_fusion
  65.3 5.3 %fusion.44 = (f32[32,16]{1,0:T(8,128)S(1)}, f32[32,16,3072]{2,1,0:T(8,128)}) fusion(s32[16]{0:T(128)S(1)} %broadcast_multiply_fusion.1, s32[32,3072]{1,0:T(8,128)S(1)} %add_multiply_fusion, bf16[32,4,3072]{2,1,0:T(4,128)(2,1)S(1)} %all_gather.9, s32[16]{0:T(128)} %bitcast.51), kind=kOutput, calls=%fused_computation.68 | convolution fusion | flops 31456960 | bytes 7473280 | tf_op jit(solution)/shard_map/si,tid->tsd/dot_general | solution.py:49
  70.7 3.5 %psum.35 = f32[32,16]{1,0:T(8,128)S(1)} all-reduce(f32[32,16]{1,0:T(8,128)S(1)} %get-tuple-element.18), channel_id=1, replica_groups=mesh['noise'=8,'row'=16,'col'=2] {'col'}, use_global_device_ids=true, to_apply=%region_1.0 | all-reduce | flops 512 | bytes 4096 | tf_op jit(solution)/shard_map/psum | solution.py:62
  74.1 3.5 %multiply_reduce_fusion.1 = f32[32,16]{1,0:T(8,128)S(1)} fusion(f32[32,16,3072]{2,1,0:T(8,128)} %get-tuple-element.19, f32[32,16]{1,0:T(8,128)S(1)} %broadcast_multiply_fusion), kind=kLoop, calls=%fused_computation.10 | loop fusion | flops 4718080 | bytes 6295552 | tf_op jit(solution)/shard_map/reduce_sum | solution.py:64
  77.7 0.0 copy-done.2
  77.7 0.0 slice-start
  77.7 3.4 %multiply_reduce_fusion = f32[768]{0:T(1024)S(1)} fusion(bf16[3072,768]{1,0:T(8,128)(2,1)} %param.9, f32[3072]{0:T(1024)S(1)} %copy-done.2), kind=kLoop, calls=%fused_computation.2 | loop fusion | flops 7077120 | bytes 4733952 | tf_op jit(solution)/shard_map/reduce_sum | solution.py:78
  81.1 3.6 %all-reduce.3 = (f32[32,16]{1,0:T(8,128)S(1)}, f32[768]{0:T(1024)S(1)}) all-reduce(f32[32,16]{1,0:T(8,128)S(1)} %multiply_reduce_fusion.1, f32[768]{0:T(1024)S(1)} %multiply_reduce_fusion), channel_id=1, replica_groups=mesh['noise'=8,'row'=16,'col'=2] {'col'}, use_global_device_ids=true, to_apply=%region_3.0 | all-reduce | flops 1280 | bytes 10240 | tf_op jit(solution)/shard_map/psum | solution.py:64
  84.7 0.0 slice-start.1
  84.7 7.3 %multiply_convert_fusion = (bf16[32,16,3072]{2,1,0:T(8,128)(2,1)S(1)}, f32[32,16,3072]{2,1,0:T(8,128)}) fusion(f32[3072]{0:T(1024)S(1)} %copy-done.2, f32[32,16]{1,0:T(8,128)S(1)} %get-tuple-element.17, f32[32,16,3072]{2,1,0:T(8,128)} %get-tuple-element.19, f32[32,16]{1,0:T(8,128)S(1)} %broadcast_multiply_fusion), kind=kLoop, calls=%fused_computation.9 | loop fusion | flops 6291456 | bytes 15745024 | tf_op jit(solution)/shard_map/convert_element_type | solution.py:67
  92.0 0.0 slice-done
  92.0 3.8 %fusion.46 = f32[512,768]{1,0:T(8,128)} fusion(bf16[512,3072]{1,0:T(8,128)(2,1)S(1)} %bitcast.48, bf16[3072,768]{1,0:T(8,128)(2,1)S(1)} %bitcast.45), kind=kOutput, calls=%fused_computation.70 | convolution fusion | flops 2415919104 | bytes 9437184 | tf_op jit(solution)/shard_map/dot_general | solution.py:69
  95.8 7.1 %fusion.45 = f32[512,768]{1,0:T(8,128)} fusion(bf16[512,3072]{1,0:T(8,128)(2,1)} %bitcast.55, bf16[768,3072]{1,0:T(8,128)(2,1)} %param.10), kind=kOutput, calls=%fused_computation.69 | convolution fusion | flops 2415919104 | bytes 9437184 | tf_op jit(solution)/shard_map/td,hd->th/dot_general | solution.py:72
  102.9 0.0 all-reduce.10.cloned.1.call-update
  102.9 0.2 all-reduce.8.cloned.1.call-start
  103.2 31.5 %all-reduce.10.cloned.1.call-done = (f32[512,768]{1,0:T(8,128)}, f32[512,768]{1,0:T(8,128)}) async-done(((f32[512,768]{1,0:T(8,128)}, f32[512,768]{1,0:T(8,128)}), (f32[512,768]{1,0:T(8,128)}, f32[512,768]{1,0:T(8,128)})) %all-reduce.10.cloned.1.call-update) | async-done | bytes 3145744 | tf_op jit(solution)/shard_map/psum | solution.py:79
  134.7 3.2 %fusion.10 = (f32[512]{0:T(512)S(1)}, f32[512]{0:T(512)S(1)}, bf16[512,768]{1,0:T(8,128)(2,1)S(1)}) fusion(f32[768]{0:T(1024)S(1)} %get-tuple-element.8, f32[512,768]{1,0:T(8,128)} %get-tuple-element.10, f32[512,768]{1,0:T(8,128)} %get-tuple-element.9), kind=kLoop, calls=%fused_computation.21 | loop fusion | flops 9436160 | bytes 3939328 | tf_op jit(solution)/shard_map/reduce_sum | solution.py:82
  137.9 0.5 convolution_convert_fusion
  138.3 0.0 copy-start.4
  138.4 0.0 copy-start.1
  138.4 4.0 %fusion.6 = f32[32,4,3072]{2,0,1:T(8,128)S(1)} fusion(bf16[3072,768]{1,0:T(8,128)(2,1)} %param.9, bf16[32,4,768]{2,1,0:T(4,128)(2,1)S(1)} %convolution_convert_fusion), kind=kOutput, calls=%fused_computation.12 | convolution fusion | flops 603979776 | bytes 6488064 | tf_op jit(solution)/shard_map/th,dh->td/dot_general | solution.py:91
  142.4 2.2 copy.20
  144.6 0.0 all-reduce.8.cloned.1.call-update
  144.7 0.6 dynamic-slice.1
  145.9 0.1 fusion.35
  146.1 0.1 stack.8
  146.1 0.1 stack.9
  146.2 69.6 %all-reduce.2 = f32[32,16,2]{1,0,2:T(8,128)S(1)} all-reduce(f32[32,16,2]{1,0,2:T(8,128)S(1)} %maximum_multiply_fusion), channel_id=3, replica_groups=mesh['noise'=8,'row'=16,'col'=2] {'row'}, use_global_device_ids=true, to_apply=%region_11.0.clone | all-reduce | flops 1024 | bytes 8192
  215.9 28.8 %all-reduce.8.cloned.1.call-done = f32[32,4,3072]{2,1,0:T(4,128)} async-done(((f32[32,4,3072]{2,1,0:T(4,128)}), f32[32,4,3072]{2,1,0:T(4,128)}) %all-reduce.8.cloned.1.call-update) | async-done | bytes 1572880
  244.7 0.0 copy-done.1
  244.7 1.4 fusion.9
  246.1 0.1 stack.11
  246.2 28.3 %all_to_all.24 = f32[8,2,4,3072]{3,2,1,0:T(4,128)S(1)} all-to-all(f32[8,2,4,3072]{3,2,1,0:T(4,128)S(1)} %stack.11), channel_id=1, replica_groups=mesh['noise'=8,'row'=16,'col'=2] {'noise'}, dimensions={0} | all-to-all | bytes 1572864 | tf_op jit(solution)/shard_map/all_to_all | solution.py:108
  274.6 0.9 copy.32
  (18 shorter events, 0.1 us)
Async XLA Ops:
  6.5 33.3 %copy-start = (bf16[16,4,3072]{2,1,0:T(4,128)(2,1)S(1)}, bf16[16,4,3072]{2,1,0:T(4,128)(2,1)}, u32[]{:S(2)}) copy-start(bf16[16,4,3072]{2,1,0:T(4,128)(2,1)} %param.7) | copy-start | bytes 1179652
  6.5 89.3 %all-gather.2.cloned.1.call-start = ((), (), s32[]{:S(2)}) async-start(), calls=%async_computation.2 | async-start | bytes 3342336 | tf_op jit(solution)/shard_map/all_gather | solution.py:45
  26.5 108.2 %all-reduce.10.cloned.1.call-start = ((), (), s32[]{:S(2)}) async-start(), calls=%async_computation.4 | async-start | bytes 6291456 | tf_op jit(solution)/shard_map/psum | solution.py:79
  70.7 7.0 %copy-start.2 = (f32[3072]{0:T(1024)S(1)}, f32[3072]{0:T(1024)}, u32[]{:S(2)}) copy-start(f32[3072]{0:T(1024)} %param.8) | copy-start | bytes 36868
  77.7 14.3 %slice-start = ((s8[4718592]{0:T(1024)(128)(4,1)}), s8[524288]{0:T(1024)(128)(4,1)S(1)}, s32[]{:S(2)}) async-start(s8[4718592]{0:T(1024)(128)(4,1)} %bitcast.44), calls=%async_computation.5 | async-start | bytes 1048576
  84.7 7.3 %slice-start.1 = ((s8[4718592]{0:T(1024)(128)(4,1)}), s8[4194304]{0:T(1024)(128)(4,1)S(1)}, s32[]{:S(2)}) async-start(s8[4718592]{0:T(1024)(128)(4,1)} %bitcast.44), calls=%async_computation.6 | async-start | bytes 8388608
  95.8 7.3 %copy-start.3 = (s32[16,1]{0,1:T(1,128)S(1)}, s32[16,1]{0,1:T(1,128)}, u32[]{:S(2)}) copy-start(s32[16,1]{0,1:T(1,128)} %param.13) | copy-start | bytes 196
  102.9 141.7 %all-reduce.8.cloned.1.call-start = ((), (), s32[]{:S(2)}) async-start(), calls=%async_computation.3 | async-start | bytes 3145728
  138.3 6.3 %copy-start.4 = (u32[256]{0:T(256)S(1)}, u32[256]{0:T(256)}, u32[]{:S(2)}) copy-start(u32[256]{0:T(256)} %constant.75) | copy-start | bytes 3076
  138.4 106.3 %copy-start.1 = (bf16[2,16,3072]{2,1,0:T(8,128)(2,1)S(1)}, bf16[2,16,3072]{2,1,0:T(8,128)(2,1)}, u32[]{:S(2)}) copy-start(bf16[2,16,3072]{2,1,0:T(8,128)(2,1)} %all_to_all.19) | copy-start | bytes 589828
Sparse Core Ops, SparseCore 0:
  26.6 49.4 all-gather.1
  103.0 31.6 all-reduce.9
  144.8 99.8 all-reduce.7
